TPU v7x, 32 devices: a whole 2x2x4 slice. The times are simulated.
32 devices in a mesh: wide: 8 (over y, x, core), narrow: 4 (over z).
Axes of the slice: x: 2, y: 2, z: 4, core: 2. Of those that a mesh axis runs over, the one named last changes fastest.
Arguments:
- images: bfloat16 [256, 24, 24, 384], P(('wide', 'narrow')), may hold values from -6 to 6
- cotangent: bfloat16 [256, 24, 24, 384], P(('wide', 'narrow')), may hold values from -6 to 6
- group_ids: int32 [256], P(('wide', 'narrow')), may hold values from 0 to 2
- keep_mask: int32 [256], P(('wide', 'narrow')), may hold values 0 or 1
- up_weight: float32 [384, 1536], P(None, ('wide', 'narrow')), may hold values from -0.3125 to 0.3125
- down_weight: float32 [1536, 384], P(('wide', 'narrow')), may hold values from -0.15625 to 0.15625
- small_params: float32 [22272], P(('wide', 'narrow')), may hold values from -1 to 1.5, as said below
- up_moment: float32 [384, 1536], P(None, ('wide', 'narrow')), may hold values from -64 to 64
- down_moment: float32 [1536, 384], P(('wide', 'narrow')), may hold values from -128 to 128
- small_moment: float32 [22272], P(('wide', 'narrow')), may hold values from -128 to 128
- up_second: float32 [384, 1536], P(None, ('wide', 'narrow')), may hold values from 10.10064 to 42.086
- down_second: float32 [1536, 384], P(('wide', 'narrow')), may hold values from 42.086 to 168.344
- small_second: float32 [22272], P(('wide', 'narrow')), may hold values from 30.30192 to 126.258
Outputs:
- activations: bfloat16 [256, 24, 24, 384], P(('wide', 'narrow'))
- input_grad: float32 [256, 24, 24, 384], P(('wide', 'narrow'))
- up_new: float32 [384, 1536], P(None, ('wide', 'narrow'))
- down_new: float32 [1536, 384], P(('wide', 'narrow'))
- small_new: float32 [22272], P(('wide', 'narrow'))
- up_first: float32 [384, 1536], P(None, ('wide', 'narrow'))
- down_first: float32 [1536, 384], P(('wide', 'narrow'))
- small_first: float32 [22272], P(('wide', 'narrow'))
- up_second_new: float32 [384, 1536], P(None, ('wide', 'narrow'))
- down_second_new: float32 [1536, 384], P(('wide', 'narrow'))
- small_second_new: float32 [22272], P(('wide', 'narrow'))
- up_copy: bfloat16 [384, 1536], P(None, ('wide', 'narrow'))
- down_copy: bfloat16 [1536, 384], P(('wide', 'narrow'))
- small_copy: bfloat16 [22272], P(('wide', 'narrow'))
Inputs may be any that keep to these rules, and one draw needn't show every extreme that they name: `small_params`: rows 0 to 48 hold depthwise taps, row 50 the norm gain and row 53 the layer scale, both positive.
All inputs are finite; a program needn't handle non-finite values. No bound on the sum of `keep_mask` on one device may be relied on, other than what follows from the above.
Results may differ from a plain program's by a relative error of at most 0.0086.
Values may be sent and summed in bfloat16 or wider, within the bound.
A program may use at most 192 MiB of HBM per device.

v0:
```python
from functools import partial

import jax
import jax.numpy as jnp
from jax import lax
from jax.sharding import PartitionSpec as P

SIDE_A = 14
SIDE_B = 18
SIDE_C = 24
STEP = 10


beta_one = 0.9
beta_two = 0.999
adam_eps = 1e-08
rate_mats = 0.02
rate_small = 0.05
decay_mats = 0.05


def side_of(group_ids):
    return jnp.where(group_ids == 0, SIDE_A, jnp.where(group_ids == 1, SIDE_B, SIDE_C)).astype(
        jnp.int32
    )


def valid_mask(sides, extent):
    places = jnp.arange(extent, dtype=jnp.int32)
    inside = (places[None, :, None] < sides[:, None, None]) & (
        places[None, None, :] < sides[:, None, None]
    )
    return inside.astype(jnp.float32)[..., None]


def inner_rows(left, right):
    return lax.dot_general(
        left, right, (((0,), (0,)), ((), ())), preferred_element_type=jnp.float32
    )


def inner_cols(left, right):
    return lax.dot_general(
        left, right, (((1,), (1,)), ((), ())), preferred_element_type=jnp.float32
    )


def adam_update(weight, moment, second, grad, rate, decay):
    first = beta_one * moment + (1.0 - beta_one) * grad
    second_new = beta_two * second + (1.0 - beta_two) * grad * grad
    step_dir = (
        first / (1.0 - beta_one**STEP) / (jnp.sqrt(second_new / (1.0 - beta_two**STEP)) + adam_eps)
    )
    return (weight - rate * (step_dir + decay * weight), first, second_new)


def per_device(
    images,
    cotangent,
    group_ids,
    keep_mask,
    up_weight,
    down_weight,
    small_params,
    up_moment,
    down_moment,
    small_moment,
    up_second,
    down_second,
    small_second,
):
    width = images.shape[3]
    extent = images.shape[1]
    hidden = 4 * width
    sent = (
        up_weight.astype(jnp.bfloat16),
        down_weight.astype(jnp.bfloat16),
        small_params.astype(jnp.bfloat16),
    )
    full_up, full_down, full_small = (
        lax.all_gather(sent[0], ("wide", "narrow"), axis=1, tiled=True),
        lax.all_gather(sent[1], ("wide", "narrow"), axis=0, tiled=True),
        lax.all_gather(sent[2], ("wide", "narrow"), axis=0, tiled=True),
    )
    rows = full_small.astype(jnp.float32).reshape(58, width)
    taps = rows[:49]
    ln_gain = rows[50]
    layer_scale = rows[53]
    valid = valid_mask(side_of(group_ids), extent)
    drop = (keep_mask.astype(jnp.float32) / 0.9)[:, None, None, None]
    inputs = images.astype(jnp.float32)
    masked = inputs * valid
    padded = jnp.pad(masked, ((0, 0), (3, 3), (3, 3), (0, 0)))
    total = jnp.zeros_like(masked)
    for tap in range(49):
        row_off, col_off = divmod(tap, 7)
        total = (
            total + taps[tap] * padded[:, row_off : row_off + extent, col_off : col_off + extent, :]
        )
    conv = total + rows[49]
    center = conv - jnp.mean(conv, axis=-1, keepdims=True)
    spread = jnp.mean(center * center, axis=-1, keepdims=True)
    inv_std = lax.rsqrt(spread + 1e-06)
    normed = center * inv_std
    act = (normed * ln_gain + rows[51]).astype(jnp.bfloat16).reshape(-1, width)
    pre = jnp.dot(act, full_up, preferred_element_type=jnp.float32) + rows[54:].reshape(hidden)
    post, gelu_pull = jax.vjp(partial(jax.nn.gelu, approximate=False), pre)
    post_low = post.astype(jnp.bfloat16)
    proj = jnp.dot(post_low, full_down, preferred_element_type=jnp.float32).reshape(masked.shape)
    shifted = proj + rows[52]
    activations = (valid * (inputs + shifted * layer_scale * drop)).astype(jnp.bfloat16)
    upstream = cotangent.astype(jnp.float32) * valid
    branch_grad = upstream * drop
    scale_grad = jnp.sum(branch_grad * shifted, axis=(0, 1, 2))
    proj_full = branch_grad * layer_scale
    outb_grad = jnp.sum(proj_full, axis=(0, 1, 2))
    proj_grad = proj_full.astype(jnp.bfloat16).reshape(-1, width)
    back_up, back_down = (
        lax.all_gather(up_weight.astype(jnp.bfloat16), ("wide", "narrow"), axis=1, tiled=True),
        lax.all_gather(down_weight.astype(jnp.bfloat16), ("wide", "narrow"), axis=0, tiled=True),
    )
    down_grad = inner_rows(post_low, proj_grad)
    post_grad = inner_cols(proj_grad, back_down)
    pre_grad = gelu_pull(post_grad)[0].astype(jnp.bfloat16)
    hid_grad = jnp.sum(pre_grad.astype(jnp.float32), axis=0)
    up_grad = inner_rows(act, pre_grad)
    act_grad = inner_cols(pre_grad, back_up).reshape(masked.shape)
    gain_grad = jnp.sum(act_grad * normed, axis=(0, 1, 2))
    normb_grad = jnp.sum(act_grad, axis=(0, 1, 2))
    norm_grad = act_grad * ln_gain
    conv_grad = inv_std * (
        norm_grad
        - jnp.mean(norm_grad, axis=-1, keepdims=True)
        - normed * jnp.mean(norm_grad * normed, axis=-1, keepdims=True)
    )
    convb_grad = jnp.sum(conv_grad, axis=(0, 1, 2))
    padded_grad = jnp.pad(conv_grad, ((0, 0), (3, 3), (3, 3), (0, 0)))
    tap_grads = []
    back_total = jnp.zeros_like(masked)
    for tap in range(49):
        row_off, col_off = divmod(tap, 7)
        window = padded[:, row_off : row_off + extent, col_off : col_off + extent, :]
        tap_grads.append(jnp.sum(conv_grad * window, axis=(0, 1, 2)))
        back_win = padded_grad[
            :, 6 - row_off : 6 - row_off + extent, 6 - col_off : 6 - col_off + extent, :
        ]
        back_total = back_total + taps[tap] * back_win
    input_grad = upstream + valid * back_total
    small_grad = jnp.concatenate(
        [
            jnp.stack(tap_grads),
            jnp.stack([convb_grad, gain_grad, normb_grad, outb_grad, scale_grad]),
            hid_grad.reshape(4, width),
        ],
        axis=0,
    ).reshape(-1)
    up_sum, down_sum, small_sum = (
        lax.psum_scatter(up_grad, ("wide", "narrow"), scatter_dimension=1, tiled=True),
        lax.psum_scatter(down_grad, ("wide", "narrow"), scatter_dimension=0, tiled=True),
        lax.psum_scatter(small_grad, ("wide", "narrow"), scatter_dimension=0, tiled=True),
    )
    up_new, up_first, up_second_new = adam_update(
        up_weight, up_moment, up_second, up_sum, rate_mats, decay_mats
    )
    down_new, down_first, down_second_new = adam_update(
        down_weight, down_moment, down_second, down_sum, rate_mats, decay_mats
    )
    small_new, small_first, small_second_new = adam_update(
        small_params, small_moment, small_second, small_sum, rate_small, 0.0
    )
    return (
        activations,
        input_grad,
        up_new,
        down_new,
        small_new,
        up_first,
        down_first,
        small_first,
        up_second_new,
        down_second_new,
        small_second_new,
        up_new.astype(jnp.bfloat16),
        down_new.astype(jnp.bfloat16),
        small_new.astype(jnp.bfloat16),
    )


def solution(mesh):
    placed = (
        P(("wide", "narrow"), None, None, None),
        P(("wide", "narrow"), None, None, None),
        P(("wide", "narrow")),
        P(("wide", "narrow")),
        P(None, ("wide", "narrow")),
        P(("wide", "narrow"), None),
        P(("wide", "narrow")),
        P(None, ("wide", "narrow")),
        P(("wide", "narrow"), None),
        P(("wide", "narrow")),
        P(None, ("wide", "narrow")),
        P(("wide", "narrow"), None),
        P(("wide", "narrow")),
    )
    return jax.shard_map(
        per_device,
        mesh=mesh,
        in_specs=placed,
        out_specs=(
            P(("wide", "narrow"), None, None, None),
            P(("wide", "narrow"), None, None, None),
            P(None, ("wide", "narrow")),
            P(("wide", "narrow"), None),
            P(("wide", "narrow")),
            P(None, ("wide", "narrow")),
            P(("wide", "narrow"), None),
            P(("wide", "narrow")),
            P(None, ("wide", "narrow")),
            P(("wide", "narrow"), None),
            P(("wide", "narrow")),
            P(None, ("wide", "narrow")),
            P(("wide", "narrow"), None),
            P(("wide", "narrow")),
        ),
        check_vma=False,
    )
```

profile of v0, /device:TPU:0, one launch (start us, length us, event | category | flops | bytes accessed | tf_op | source)
XLA Modules:
  0.0 962.0 jit_solution(13442284881792773211)
XLA Ops:
  7.2 1.5 convert_element_type.65
  8.8 1.5 convert_element_type.67
  11.3 42.5 %all-reduce.2 = bf16[22272]{0:T(1024)(128)(2,1)S(1)} all-reduce(bf16[22272]{0:T(1024)(128)(2,1)S(1)} %dynamic-update-slice), channel_id=1, replica_groups=mesh['wide'=8,'narrow'=4] {'wide','narrow'}, use_global_device_ids=true, to_apply=%add.2 | all-reduce | flops 22272 | bytes 89088
  57.5 4.8 convert_multiply_fusion
  62.3 201.9 %fusion.122 = (f32[8,24,24]{2,1,0:T(8,128)S(1)}, f32[8,24,24,384]{3,2,1,0:T(8,128)}) fusion(f32[384]{0:T(512)S(1)} %get-tuple-element.154, f32[384]{0:T(512)} %get-tuple-element.153, f32[384]{0:T(512)} %get-tuple-element.152, f32[384]{0:T(512)} %get-tuple-element.151, f32[384]{0:T(512)} %get-tuple-element.150, f32[384]{0:T(512)} %get-tuple-element.149, ...), kind=kLoop, calls=%fused_computation.305 | loop fusion | flops 175173120 | bytes 14251008 | tf_op jit(solution)/shard_map/reduce_sum | solution.py:101
  264.7 4.2 multiply_reduce_fusion.53
  269.8 1.5 add_convert_fusion.1
  271.3 69.4 %multiply_convert_fusion = (bf16[4608,1536]{1,0:T(8,128)(2,1)}, f32[4608,1536]{1,0:T(8,128)}, f32[4608,1536]{1,0:T(8,128)}) fusion(f32[1536]{0:T(1024)} %slice.862, bf16[4608,384]{1,0:T(8,128)(2,1)S(1)} %bitcast.21, bf16[384,1536]{0,1:T(8,128)(2,1)} %all-gather.3.cloned.1.call-done), kind=kOutput, calls=%fused_computation.100 | convolution fusion | flops 5902958592 | bytes 75503616 | tf_op jit(solution)/shard_map/dot_general | solution.py:106
  340.8 10.8 %fusion.126 = f32[4608,384]{1,0:T(8,128)S(1)} fusion(bf16[4608,1536]{1,0:T(8,128)(2,1)} %get-tuple-element.95, bf16[1536,384]{1,0:T(8,128)(2,1)} %all-gather.5.cloned.1.call-done), kind=kOutput, calls=%fused_computation.309 | convolution fusion | flops 5435817984 | bytes 22413312 | tf_op jit(solution)/shard_map/dot_general | solution.py:109
  351.7 4.5 multiply_reduce_fusion
  356.2 28.9 %convert_reduce_fusion = (f32[1536]{0:T(1024)}, bf16[4608,1536]{1,0:T(8,128)(2,1)}) fusion(f32[4608,1536]{1,0:T(8,128)} %get-tuple-element.96, bf16[4608,384]{1,0:T(8,128)(2,1)S(1)} %bitcast.23, bf16[1536,384]{1,0:T(8,128)(2,1)} %all-gather.5.cloned.1.call-done, f32[4608,1536]{1,0:T(8,128)} %get-tuple-element.155, f32[1536]{0:T(1024)} %slice.862), kind=kOutput, calls=%fused_computation.98 | convolution fusion | flops 5556140544 | bytes 75509760 | tf_op jit(solution)/shard_map/dot_general | solution.py:43
  385.1 11.5 %fusion.113 = (f32[384]{0:T(512)}, f32[4608]{0:T(1024)S(1)}, f32[4608,384]{1,0:T(8,128)S(1)}) fusion(f32[384]{0:T(512)S(1)} %copy-done.17, bf16[4608,1536]{1,0:T(8,128)(2,1)} %get-tuple-element.158, bf16[384,1536]{0,1:T(8,128)(2,1)} %all-gather.3.cloned.1.call-done), kind=kOutput, calls=%fused_computation.300 | convolution fusion | flops 5441121280 | bytes 22434816 | tf_op jit(solution)/shard_map/dot_general | solution.py:43
  396.6 7.6 multiply_reduce_fusion.1
  404.4 73.9 %multiply_reduce_fusion.2 = (f32[384]{0:T(512)}, f32[384]{0:T(512)}, f32[384]{0:T(512)}, f32[384]{0:T(512)}, f32[384]{0:T(512)}, /*index=5*/f32[384]{0:T(512)}, ...) fusion(f32[8,24,24,384]{3,2,1,0:T(8,128)} %convert_multiply_fus, ...), kind=kLoop, calls=%fused_computation.218 | loop fusion | flops 76080384 | bytes 28414464 | tf_op jit(solution)/shard_map/reduce_sum | solution.py:143
  478.3 16.6 %fusion.114 = (f32[384]{0:T(512)}, f32[384]{0:T(512)}, f32[384]{0:T(512)}, f32[384]{0:T(512)}, f32[384]{0:T(512)}, /*index=5*/f32[384]{0:T(512)}, f32[384]{0:T(5...) fusion(f32[8,24,24,384]{3,2,1,0:T(8,128)} %get-tuple-element.94, ...), kind=kLoop, calls=%fused_computation.301 | loop fusion | flops 51309312 | bytes 17734656 | tf_op jit(solution)/shard_map/reduce_sum | solution.py:136
  495.0 53.9 %multiply_reduce_fusion.20 = (f32[384]{0:T(512)}, f32[384]{0:T(512)}, f32[384]{0:T(512)}, f32[384]{0:T(512)}, f32[384]{0:T(512)}, /*index=5*/f32[384]{0:T(512)},...) fusion(f32[8,24,24,384]{3,2,1,0:T(8,128)} %get-tuple-element.94, ...), kind=kLoop, calls=%fused_computation.236 | loop fusion | flops 63694080 | bytes 14183424 | tf_op jit(solution)/shard_map/reduce_sum | solution.py:143
  548.8 1.3 stack.162
  570.2 1.3 stack.178
  577.4 1.3 stack.184
  578.7 1.3 stack.185
  579.9 1.3 stack.187
  608.9 1.3 stack.213
  611.5 10.6 %concatenate.3 = f32[58,384]{1,0:T(8,128)} concatenate(f32[1,384]{1,0:T(1,128)} %stack.162, f32[1,384]{1,0:T(1,128)} %stack.163, f32[1,384]{1,0:T(1,128)} %stack.164, f32[1,384]{1,0:T(1,128)} %stack.165, f32[1,384]{1,0:T(1,128)} %stack.166, f32[1,384]{1,0:T(1,128)} %stack.167, f32[1,384]{1,0:T(1,128)} %stack.168, f32[1,384]{1,0:T(1,128)} %stack.169, f32[1,384]{1,0:T(1,128)} %stack.170, ...), dimensions={0} | concatenate | bytes 178176 | tf_op jit(solution)/shard_map/concatenate | solution.py:149
  622.1 1.5 reshape.292
  623.7 11.7 %fusion.128 = f32[1536,384]{1,0:T(8,128)} fusion(bf16[4608,1536]{1,0:T(8,128)(2,1)} %get-tuple-element.95, bf16[4608,384]{1,0:T(8,128)(2,1)S(1)} %bitcast.24), kind=kOutput, calls=%fused_computation.311 | convolution fusion | flops 5435817984 | bytes 20054016 | tf_op jit(solution)/shard_map/dot_general | solution.py:37
  635.6 13.2 %fusion.127 = f32[384,1536]{0,1:T(8,128)} fusion(bf16[4608,384]{1,0:T(8,128)(2,1)} %bitcast.22, bf16[4608,1536]{1,0:T(8,128)(2,1)} %get-tuple-element.158), kind=kOutput, calls=%fused_computation.310 | convolution fusion | flops 5435817984 | bytes 20054016 | tf_op jit(solution)/shard_map/dot_general | solution.py:37
  648.9 180.7 %fusion.102 = f32[8,24,24,384]{3,2,1,0:T(8,128)} fusion(f32[8,24,24,384]{3,2,1,0:T(8,128)} %get-tuple-element.94, bf16[8,24,24,384]{3,2,1,0:T(8,128)(2,1)S(1)} %copy-done.5, f32[384]{0:T(512)} %get-tuple-element.153, f32[384]{0:T(512)} %get-tuple-element.152, f32[384]{0:T(512)} %get-tuple-element.151, f32[384]{0:T(512)} %get-tuple-element.150, ...), kind=kLoop, calls=%fused_computation.212 | loop fusion | flops 178716672 | bytes 17788416 | tf_op jit(solution)/shard_map/add | solution.py:148
  829.6 1.4 fusion.115
  831.1 18.2 %reduce-scatter.5.cloned.1.call-done = f32[48,384]{1,0:T(8,128)} async-done(((f32[1536,384]{1,0:T(8,128)}), f32[48,384]{1,0:T(8,128)}) %reduce-scatter.5.cloned.1.call-update) | async-done | bytes 73744 | tf_op jit(solution)/shard_map/reduce_scatter | solution.py:159
  849.2 1.7 fusion.117
  851.0 102.3 %reduce-scatter.3.cloned.1.call-done = f32[384,48]{0,1:T(8,128)} async-done(((f32[384,1536]{0,1:T(8,128)}), f32[384,48]{0,1:T(8,128)}) %reduce-scatter.3.cloned.1.call-update) | async-done | bytes 73744 | tf_op jit(solution)/shard_map/reduce_scatter | solution.py:158
  953.3 1.7 fusion.119
  (211 shorter events, 60.9 us)
Async XLA Ops:
  7.2 264.2 %all-gather.3.cloned.1.call-start = ((), (), s32[]{:S(2)}) async-start(), calls=%async_computation.2 | async-start | bytes 1216512 | tf_op jit(solution)/shard_map/all_gather | solution.py:81
  8.8 332.0 %all-gather.5.cloned.1.call-start = ((), (), s32[]{:S(2)}) async-start(), calls=%async_computation.3 | async-start | bytes 1216512 | tf_op jit(solution)/shard_map/all_gather | solution.py:82
  10.3 819.3 %all-reduce.6.cloned.1.call-start = ((), (), s32[]{:S(2)}) async-start(), calls=%async_computation.6 | async-start | bytes 180224
  54.4 209.9 %copy-start.18 = (f32[384]{0:T(512)}, f32[384]{0:T(512)S(1)}, u32[]{:S(2)}) copy-start(f32[384]{0:T(512)S(1)} %get-tuple-element.105) | copy-start | bytes 4612
  54.4 209.9 %copy-start.20 = (f32[384]{0:T(512)}, f32[384]{0:T(512)S(1)}, u32[]{:S(2)}) copy-start(f32[384]{0:T(512)S(1)} %get-tuple-element.106) | copy-start | bytes 4612
  54.4 209.9 %copy-start.22 = (f32[384]{0:T(512)}, f32[384]{0:T(512)S(1)}, u32[]{:S(2)}) copy-start(f32[384]{0:T(512)S(1)} %get-tuple-element.107) | copy-start | bytes 4612
  54.4 209.9 %copy-start.24 = (f32[384]{0:T(512)}, f32[384]{0:T(512)S(1)}, u32[]{:S(2)}) copy-start(f32[384]{0:T(512)S(1)} %get-tuple-element.108) | copy-start | bytes 4612
  54.4 209.9 %copy-start.26 = (f32[384]{0:T(512)}, f32[384]{0:T(512)S(1)}, u32[]{:S(2)}) copy-start(f32[384]{0:T(512)S(1)} %get-tuple-element.109) | copy-start | bytes 4612
  54.4 209.9 %copy-start.27 = (f32[384]{0:T(512)}, f32[384]{0:T(512)S(1)}, u32[]{:S(2)}) copy-start(f32[384]{0:T(512)S(1)} %get-tuple-element.110) | copy-start | bytes 4612
  54.4 209.9 %copy-start.28 = (f32[384]{0:T(512)}, f32[384]{0:T(512)S(1)}, u32[]{:S(2)}) copy-start(f32[384]{0:T(512)S(1)} %get-tuple-element.111) | copy-start | bytes 4612
  54.5 209.9 %copy-start.29 = (f32[384]{0:T(512)}, f32[384]{0:T(512)S(1)}, u32[]{:S(2)}) copy-start(f32[384]{0:T(512)S(1)} %get-tuple-element.112) | copy-start | bytes 4612
  54.5 209.9 %copy-start.30 = (f32[384]{0:T(512)}, f32[384]{0:T(512)S(1)}, u32[]{:S(2)}) copy-start(f32[384]{0:T(512)S(1)} %get-tuple-element.113) | copy-start | bytes 4612
  54.5 209.9 %copy-start.31 = (f32[384]{0:T(512)}, f32[384]{0:T(512)S(1)}, u32[]{:S(2)}) copy-start(f32[384]{0:T(512)S(1)} %get-tuple-element.114) | copy-start | bytes 4612
  54.5 209.9 %copy-start.32 = (f32[384]{0:T(512)}, f32[384]{0:T(512)S(1)}, u32[]{:S(2)}) copy-start(f32[384]{0:T(512)S(1)} %get-tuple-element.115) | copy-start | bytes 4612
  54.5 209.9 %copy-start.33 = (f32[384]{0:T(512)}, f32[384]{0:T(512)S(1)}, u32[]{:S(2)}) copy-start(f32[384]{0:T(512)S(1)} %get-tuple-element.116) | copy-start | bytes 4612
  54.5 209.9 %copy-start.34 = (f32[384]{0:T(512)}, f32[384]{0:T(512)S(1)}, u32[]{:S(2)}) copy-start(f32[384]{0:T(512)S(1)} %get-tuple-element.117) | copy-start | bytes 4612
  54.5 209.9 %copy-start.35 = (f32[384]{0:T(512)}, f32[384]{0:T(512)S(1)}, u32[]{:S(2)}) copy-start(f32[384]{0:T(512)S(1)} %get-tuple-element.118) | copy-start | bytes 4612
  54.5 209.9 %copy-start.36 = (f32[384]{0:T(512)}, f32[384]{0:T(512)S(1)}, u32[]{:S(2)}) copy-start(f32[384]{0:T(512)S(1)} %get-tuple-element.119) | copy-start | bytes 4612
  54.5 215.0 %copy-start.16 = (f32[384]{0:T(512)}, f32[384]{0:T(512)S(1)}, u32[]{:S(2)}) copy-start(f32[384]{0:T(512)S(1)} %get-tuple-element.103) | copy-start | bytes 4612
  54.6 209.9 %copy-start.37 = (f32[384]{0:T(512)}, f32[384]{0:T(512)S(1)}, u32[]{:S(2)}) copy-start(f32[384]{0:T(512)S(1)} %get-tuple-element.120) | copy-start | bytes 4612
  54.6 209.9 %copy-start.38 = (f32[384]{0:T(512)}, f32[384]{0:T(512)S(1)}, u32[]{:S(2)}) copy-start(f32[384]{0:T(512)S(1)} %get-tuple-element.121) | copy-start | bytes 4612
  54.6 209.9 %copy-start.39 = (f32[384]{0:T(512)}, f32[384]{0:T(512)S(1)}, u32[]{:S(2)}) copy-start(f32[384]{0:T(512)S(1)} %get-tuple-element.122) | copy-start | bytes 4612
  54.6 209.9 %copy-start.40 = (f32[384]{0:T(512)}, f32[384]{0:T(512)S(1)}, u32[]{:S(2)}) copy-start(f32[384]{0:T(512)S(1)} %get-tuple-element.123) | copy-start | bytes 4612
  54.6 209.9 %copy-start.41 = (f32[384]{0:T(512)}, f32[384]{0:T(512)S(1)}, u32[]{:S(2)}) copy-start(f32[384]{0:T(512)S(1)} %get-tuple-element.124) | copy-start | bytes 4612
  54.6 209.9 %copy-start.42 = (f32[384]{0:T(512)}, f32[384]{0:T(512)S(1)}, u32[]{:S(2)}) copy-start(f32[384]{0:T(512)S(1)} %get-tuple-element.125) | copy-start | bytes 4612
  54.6 209.9 %copy-start.43 = (f32[384]{0:T(512)}, f32[384]{0:T(512)S(1)}, u32[]{:S(2)}) copy-start(f32[384]{0:T(512)S(1)} %get-tuple-element.126) | copy-start | bytes 4612
  54.6 209.9 %copy-start.44 = (f32[384]{0:T(512)}, f32[384]{0:T(512)S(1)}, u32[]{:S(2)}) copy-start(f32[384]{0:T(512)S(1)} %get-tuple-element.127) | copy-start | bytes 4612
  54.6 209.9 %copy-start.45 = (f32[384]{0:T(512)}, f32[384]{0:T(512)S(1)}, u32[]{:S(2)}) copy-start(f32[384]{0:T(512)S(1)} %get-tuple-element.128) | copy-start | bytes 4612
  54.7 209.9 %copy-start.46 = (f32[384]{0:T(512)}, f32[384]{0:T(512)S(1)}, u32[]{:S(2)}) copy-start(f32[384]{0:T(512)S(1)} %get-tuple-element.129) | copy-start | bytes 4612
  54.7 209.9 %copy-start.47 = (f32[384]{0:T(512)}, f32[384]{0:T(512)S(1)}, u32[]{:S(2)}) copy-start(f32[384]{0:T(512)S(1)} %get-tuple-element.130) | copy-start | bytes 4612
  623.6 225.6 %reduce-scatter.5.cloned.1.call-start = ((), (), s32[]{:S(2)}) async-start(), calls=%async_computation.5 | async-start | bytes 2433024 | tf_op jit(solution)/shard_map/reduce_scatter | solution.py:159
  635.5 317.8 %reduce-scatter.3.cloned.1.call-start = ((), (), s32[]{:S(2)}) async-start(), calls=%async_computation.4 | async-start | bytes 2433024 | tf_op jit(solution)/shard_map/reduce_scatter | solution.py:158
  (39 other events, 3156.5 us)
Sparse Core Ops, SparseCore 0:
  11.4 56.7 all-gather.2
  71.6 53.0 all-gather.4
  623.8 119.9 all-reduce.5
  748.9 100.2 reduce-scatter.4
  855.2 98.0 reduce-scatter.2
where the time goes:
time: 973 us; the launch traced here: 962 us
  other arithmetic  560 us (58%)
  matrix products  146 us (15%)
  waiting for transfers between devices  121 us (12%)
  local copies, waits for them, and re-layouts  78.1 us (8%)
  blocking collectives  42.5 us (4%)
  between operations  15.3 us (2%)
    reduce_sum x1, other arithmetic, per_device(): center = conv - jnp.mean(conv, axis=-1, keepdims=True)  202 us
    add x1, other arithmetic, per_device(): input_grad = upstream + valid * back_total  181 us
    reduce_sum x2, other arithmetic, per_device(): tap_grads.append(jnp.sum(conv_grad * window, axis=(0, 1, 2)))  128 us
    reduce_scatter x1, waiting for transfers between devices, per_device(): lax.psum_scatter(up_grad, ('wide', 'narrow'), scatter_dimension=1, tiled=...  102 us
    dot_general x1, matrix products, per_device(): jnp.dot(act, full_up, preferred_element_type=jnp.float32)  69.4 us
    another operation x49, local copies, waits for them, and re-layouts, per_device(): jnp.stack(tap_grads)  58.4 us
    unnamed x1, blocking collectives  42.5 us
    dot_general x2, matrix products, inner_cols(): lax.dot_general(left, right, (((1,), (1,)), ((), ())), preferred_element_...  40.4 us
  transfers between devices with their start and end apart: 5, of which 2 were waited for; matrix products, arithmetic and copies ran while one was open for 52% of the time, Pallas kernels for 0%

commit v1 on v0

v1 whole, which is shorter than its diff:
```python
from functools import partial

import jax
import jax.numpy as jnp
import ml_dtypes
import numpy as np
from jax import lax
from jax.experimental import pallas as pl
from jax.experimental.pallas import tpu as pltpu
from jax.sharding import PartitionSpec as P

SIDES = (14, 18, 24)
STEP = 10
BLOCK = 256
CHUNK = 256
VMEM_LIMIT = 60 * 1024 * 1024

beta_one = 0.9
beta_two = 0.999
adam_eps = 1e-08
rate_mats = 0.02
rate_small = 0.05
decay_mats = 0.05

BF = jnp.bfloat16
F32 = jnp.float32


def strips(total, step):
    return [(at, min(step, total - at)) for at in range(0, total, step)]


def round_up(value, step):
    return -(-value // step) * step


def make_tables(side, extent, rows):
    n = side + 3
    half = n // 2
    freqs = [(0, 0)] + [(0, v) for v in range(1, half + 1)]
    freqs += [(u, v) for u in range(1, half + 1) for v in range(n)]
    freqs = np.array(freqs, np.float64)
    count = len(freqs)
    compact = round_up(side * side, 16)
    wide = side * extent
    weight = (np.where(np.arange(count) == 0, 1.0, 2.0) / (n * n))[:, None]

    def angle(points):
        return 2.0 * np.pi / n * (freqs @ points.T)

    def stacked(top, bottom, offset):
        out = np.zeros((2 * offset, top.shape[1]), np.float64)
        out[:count] = top
        out[offset : offset + count] = bottom
        return out

    def widened(matrix, columns, spots):
        out = np.zeros((matrix.shape[0], columns), np.float64)
        out[:, spots] = matrix
        return out

    theta = angle(np.array([(i, j) for i in range(side) for j in range(side)], np.float64))
    shift = angle(np.array([(p - 3, q - 3) for p in range(7) for q in range(7)], np.float64))
    dense = np.arange(side * side)
    place = np.array([i * extent + j for i in range(side) for j in range(side)])
    own = round_up(count, 16)
    into = np.cos(theta), -np.sin(theta)
    back = weight * np.cos(theta), -weight * np.sin(theta)
    pick = np.zeros((compact, wide), np.float64)
    pick[dense, place] = 1.0
    return dict(
        freq=own,
        compact=compact,
        wide=wide,
        first_into=widened(stacked(*into, rows), extent * extent, place),
        first_back=np.pad(widened(stacked(*back, rows), compact, dense).T, ((0, extent * extent - compact), (0, 0))),
        first_taps=stacked(np.cos(shift), np.sin(shift), rows),
        into=widened(stacked(*into, own), compact, dense),
        back=widened(stacked(*back, own), wide, place).T,
        taps=np.pad(stacked(weight * np.cos(shift), -weight * np.sin(shift), own).T, ((0, 15), (0, 0))),
        pick=pick,
        spread=pick.T,
    )


def low_table(table):
    spare = round_up(table.shape[-1], 128) - table.shape[-1]
    return np.pad(table, ((0, 0),) * (table.ndim - 1) + ((0, spare),)).astype(ml_dtypes.bfloat16)


def split_table(table):
    high = table.astype(ml_dtypes.bfloat16)
    return low_table(high), low_table(table - high.astype(np.float64))


def stacked_split(table):
    pad = ((0, 0), (0, 0), (0, 64 - table.shape[2]))
    high = table.astype(ml_dtypes.bfloat16).astype(np.float64)
    return low_table(np.concatenate([np.pad(high, pad), np.pad(table - high, pad)], axis=2))


def spectrum_rows(extent):
    return round_up(((extent + 3) ** 2 + 1) // 2, 16)


def dot(left, right):
    return jnp.dot(left, right, preferred_element_type=F32)


def fold8(value):
    return jnp.sum(value.reshape(value.shape[0] // 8, 8, value.shape[1]), axis=0)


def twice_gelu(pre):
    part = pre * 0.7071067811865476
    level = 1.0 + lax.erf(part)
    bell = (pre * 0.7978845608028654) * jnp.exp2(part * part * -1.4426950408889634)
    return pre * level, level + bell


def dot_t(left, right):
    return lax.dot_general(left, right, (((1,), (1,)), ((), ())), preferred_element_type=F32)


def block_kernel(shapes, names, rows_f, extent, count, span, *refs):
    refs = list(refs)

    def take(number):
        got = refs[:number]
        del refs[:number]
        return got

    gid, keep = take(2)
    img_hbm, cot_hbm, act_far, normed_far, inv_far, spec_far, taps_far, up_far, down_far, rows = take(10)
    far_tables = [take(len(group)) for group in names]
    act_hbm, ig_hbm, up_out, down_out, small_out = take(5)
    img, cot, act_rows, normed_rows, inv_rows, cot_rows, spectra, taps_f = take(8)
    up_t, down, up_grad, down_grad, up_low, down_low = take(6)
    act_out, ig_out, work_a, work_b, prod = take(5)
    post_s, prg_s, act_t, pg_s, pg_t, eye, sums8, small = take(8)
    near_tables = [take(len(group)) for group in names]
    tables = [dict(zip(group, near)) for group, near in zip(names, near_tables)]
    cross = take(3)
    sem_img, sem_cot, sem_rows, sem_spec, sem_once, sem_out, sem_tables = take(7)

    images, pixels, width = img.shape
    hidden = up_t.shape[0]
    drop = float(np.float32(1.0) / np.float32(0.9))
    out_bias, scale, gain = rows[52:53, :], rows[53:54, :], rows[50:51, :]

    def group_of(b, s):
        if s == 0:
            return gid[b] == 0
        if s == 1:
            return gid[b] == 1
        return (gid[b] != 0) & (gid[b] != 1)

    def rows_of(b):
        sizes = [shape[1] for shape in shapes]
        size = jnp.where(gid[b] == 0, sizes[0], jnp.where(gid[b] == 1, sizes[1], sizes[2]))
        return jnp.where(keep[b] != 0, size, 0)

    def row_copies(b, off, compact):
        base = pl.multiple_of(off, 16)
        pairs = ((act_far, act_rows), (normed_far, normed_rows), (inv_far, inv_rows))
        return [
            pltpu.make_async_copy(
                far.at[b, pl.ds(0, compact)], near.at[pl.ds(base, compact)], sem_rows.at[k, b]
            )
            for k, (far, near) in enumerate(pairs)
        ]

    def cot_copy(b):
        return pltpu.make_async_copy(cot_hbm.at[b], cot.at[b], sem_cot.at[b])

    def img_copy(b):
        return pltpu.make_async_copy(img_hbm.at[b], img.at[b], sem_img.at[b])

    def spec_copy(b):
        return pltpu.make_async_copy(spec_far.at[b], spectra.at[b], sem_spec.at[b])

    mat_copies = [
        pltpu.make_async_copy(up_far, up_t, sem_once.at[0]),
        pltpu.make_async_copy(down_far, down, sem_once.at[1]),
    ]
    taps_copy = pltpu.make_async_copy(taps_far, taps_f, sem_once.at[2])
    grad_copies = [
        pltpu.make_async_copy(up_low, up_out, sem_once.at[3]),
        pltpu.make_async_copy(down_low, down_out, sem_once.at[4]),
    ]
    table_copies = []
    for s in range(3):
        for far, near in zip(far_tables[s], near_tables[s]):
            table_copies.append(
                pltpu.make_async_copy(far, near, sem_tables.at[len(table_copies)])
            )
    early = [k for k, name in enumerate(name for group in names for name in group) if name == "pick"]
    late = [k for k in range(len(table_copies)) if k not in early]

    for copy in mat_copies:
        copy.start()
    for k in early:
        table_copies[k].start()

    def fetch(b, off):
        cot_copy(b).start()
        for s in range(3):

            @pl.when((keep[b] != 0) & group_of(b, s))
            def _():
                for copy in row_copies(b, off, shapes[s][1]):
                    copy.start()

        return off + rows_of(b)

    total = lax.fori_loop(0, images, fetch, jnp.int32(0))
    up_grad[...] = jnp.zeros_like(up_grad)
    down_grad[...] = jnp.zeros_like(down_grad)
    first_row = lax.broadcasted_iota(jnp.int32, (16, BLOCK), 0) == 0
    act_t[width:, :] = jnp.where(first_row, 1.0, 0.0).astype(BF)
    same = lax.broadcasted_iota(jnp.int32, (CHUNK, CHUNK), 0) == lax.broadcasted_iota(
        jnp.int32, (CHUNK, CHUNK), 1
    )
    eye[...] = jnp.where(same, 1.0, 0.0).astype(BF)
    sums8[...] = jnp.zeros_like(sums8)
    for s in range(3):
        cross[s][...] = jnp.zeros_like(cross[s])
    end = pl.multiple_of(total, 16)
    act_rows[pl.ds(end, BLOCK), :] = jnp.zeros((BLOCK, width), BF)
    cot_rows[pl.ds(end, BLOCK), :] = jnp.zeros((BLOCK, width), BF)
    normed_rows[pl.ds(end, BLOCK), :] = jnp.zeros((BLOCK, width), BF)
    inv_rows[pl.ds(end, BLOCK), :] = jnp.zeros((BLOCK, 128), F32)
    for copy in mat_copies:
        copy.wait()
    for k in early:
        table_copies[k].wait()

    def middle(k, carry):
        base = pl.multiple_of(k * BLOCK, BLOCK)
        here = pl.ds(base, BLOCK)
        act = act_rows[here, :]
        act_t[0:width, :] = act.T
        pg_s[...] = (cot_rows[here, :].astype(F32) * (scale * drop)).astype(BF)
        pg_t[...] = pg_s[...].T
        for h in range(0, hidden, CHUNK):
            cols = slice(h, h + CHUNK)
            pre_all = dot_t(act, up_t[cols, :])
            back_all = dot_t(pg_s[...], down[cols, :])
            bias = small_bias(rows, h, CHUNK, width)
            for r, size in strips(BLOCK, 64):
                span = slice(r, r + size)
                post, slope = twice_gelu(pre_all[span] + bias)
                post_s[span, cols] = post.astype(BF)
                pull = back_all[span] * slope
                prg_s[span, cols] = pull.astype(BF)
        proj = dot(post_s[...], down[...])
        act_grad = dot(prg_s[...], up_t[...])
        for h in range(0, hidden, CHUNK):
            cols = slice(h, h + CHUNK)
            down_grad[:, cols] += dot(pg_t[...], post_s[:, cols])
            up_grad[:, cols] += dot(act_t[...], prg_s[:, cols])
        s_convb = sums8[0:8, :]
        s_gain = sums8[8:16, :]
        s_normb = sums8[16:24, :]
        s_cot = sums8[24:32, :]
        s_scale = sums8[32:40, :]
        for r, size in strips(BLOCK, 64):
            spot = pl.ds(base + r, size)
            shifted = proj[r : r + size] + 2.0 * out_bias
            arriving = cot_rows[spot, :].astype(F32)
            s_cot = s_cot + fold8(arriving)
            s_scale = s_scale + fold8(arriving * shifted)
            cot_rows[spot, :] = (shifted * (scale * (0.5 * drop))).astype(BF)
            grad = act_grad[r : r + size]
            normed = normed_rows[spot, :].astype(F32)
            s_gain = s_gain + fold8(grad * normed)
            s_normb = s_normb + fold8(grad)
            pulled = grad * (0.5 * gain)
            along = jnp.mean(pulled * normed, axis=1, keepdims=True)
            level = jnp.mean(pulled, axis=1, keepdims=True)
            inv = jnp.concatenate([inv_rows[spot, :]] * (width // 128), axis=1)
            conv_grad = inv * (pulled - level - normed * along)
            s_convb = s_convb + fold8(conv_grad)
            act_rows[spot, :] = conv_grad.astype(BF)
        sums8[0:8, :] = s_convb
        sums8[8:16, :] = s_gain
        sums8[16:24, :] = s_normb
        sums8[24:32, :] = s_cot
        sums8[32:40, :] = s_scale
        return carry

    def arrive(b, off):
        @pl.when(b < images)
        def _():
            cot_copy(b).wait()
            for s in range(3):
                _, compact, _, wide = shapes[s]

                @pl.when((keep[b] != 0) & group_of(b, s))
                def _():
                    base = pl.multiple_of(off, 16)
                    for copy in row_copies(b, off, compact):
                        copy.wait()
                    if wide < pixels:
                        cot_rows[pl.ds(base, compact), :] = dot(
                            tables[s]["pick"][:, 0:wide], cot[b, 0:wide, :]
                        ).astype(BF)
                    else:
                        cot_rows[pl.ds(base, compact), :] = cot[b]

            @pl.when(b == 1)
            def _():
                for k in late:
                    table_copies[k].start()
                taps_copy.start()
                for each in range(images):
                    spec_copy(each).start()
                    img_copy(each).start()

        inner = jnp.minimum(b, images - 1)
        after = off + jnp.where(b < images, rows_of(inner), BLOCK - 1)
        lax.fori_loop(off // BLOCK, after // BLOCK, middle, 0)
        return after

    lax.fori_loop(0, images + 1, arrive, jnp.int32(0))
    for h in range(0, hidden, CHUNK):
        cols = slice(h, h + CHUNK)
        up_low[cols, :] = dot_t(eye[...], (0.5 * up_grad[0:width, cols]).astype(BF)).astype(BF)
        down_low[cols, :] = dot_t(eye[...], (0.5 * down_grad[:, cols]).astype(BF)).astype(BF)
    for copy in grad_copies:
        copy.start()
    for k in late:
        table_copies[k].wait()
    taps_copy.wait()

    def out_copies(b, slot):
        return (
            pltpu.make_async_copy(act_out.at[slot], act_hbm.at[b], sem_out.at[0, slot]),
            pltpu.make_async_copy(ig_out.at[slot], ig_hbm.at[b], sem_out.at[1, slot]),
        )

    def last(b, off):
        slot = lax.rem(b, 2)
        img_copy(b).wait()
        spec_copy(b).wait()

        @pl.when(b >= 2)
        def _():
            for copy in out_copies(b - 2, slot):
                copy.wait()

        for s in range(3):
            side, compact, freq, wide = shapes[s]
            table = tables[s]
            inside = lax.broadcasted_iota(jnp.int32, (extent, width), 0) < side

            @pl.when((keep[b] != 0) & group_of(b, s))
            def _():
                base = pl.multiple_of(off, 16)
                work_a[0 : 2 * freq, :] = dot(
                    table["into"][:, 0:compact], act_rows[pl.ds(base, compact), :]
                )
                for r, size in strips(freq, 48):
                    lo, hi = slice(r, r + size), slice(freq + r, freq + r + size)
                    far = slice(rows_f + r, rows_f + r + size)
                    re, im = work_a[lo, :], work_a[hi, :]
                    x_re, x_im = spectra[b, lo, :].astype(F32), spectra[b, far, :].astype(F32)
                    cross[s][lo, :] += x_re * re + x_im * im
                    cross[s][hi, :] += x_im * re - x_re * im
                    t_re, t_im = taps_f[s, lo, :], taps_f[s, far, :]
                    prod[lo, :] = (re * t_re + im * t_im).astype(BF)
                    prod[hi, :] = (im * t_re - re * t_im).astype(BF)
                work_b[0:wide, :] = dot(table["back"][:, 0 : 2 * freq], prod[0 : 2 * freq, :])
                if wide < pixels:
                    work_a[0:wide, :] = dot(
                        table["spread"][:, 0:compact], cot_rows[pl.ds(base, compact), :]
                    )
                for r, size in strips(wide, extent if wide < pixels else 48):
                    spot = slice(r, r + size)
                    arriving = cot[b, spot, :].astype(F32)
                    value = img[b, spot, :].astype(F32)
                    if wide < pixels:
                        arriving = jnp.where(inside, arriving, 0.0)
                        value = jnp.where(inside, value, 0.0)
                        branch = work_a[spot, :]
                    else:
                        branch = cot_rows[pl.ds(base + r, size), :].astype(F32)
                    ig_out[slot, spot, :] = arriving + work_b[spot, :]
                    act_out[slot, spot, :] = (value + branch).astype(BF)

            @pl.when((keep[b] == 0) & group_of(b, s))
            def _():
                for i in range(side):
                    spot = slice(i * extent, (i + 1) * extent)
                    arriving = jnp.where(inside, cot[b, spot, :].astype(F32), 0.0)
                    ig_out[slot, spot, :] = arriving
                    value = jnp.where(inside, img[b, spot, :].astype(F32), 0.0)
                    act_out[slot, spot, :] = value.astype(BF)

            if wide < pixels:

                @pl.when(group_of(b, s))
                def _():
                    ig_out[slot, wide:, :] = jnp.zeros((pixels - wide, width), F32)
                    act_out[slot, wide:, :] = jnp.zeros((pixels - wide, width), BF)

        for copy in out_copies(b, slot):
            copy.start()
        return off + rows_of(b)

    lax.fori_loop(0, images, last, jnp.int32(0))

    taps_grad = jnp.zeros((64, width), F32)
    for s in range(3):
        freq = shapes[s][2]
        whole = cross[s][...]
        high = whole.astype(BF)
        rest = (whole - high.astype(F32)).astype(BF)
        taps_hi = tables[s]["taps_hi"][:, 0 : 2 * freq]
        taps_lo = tables[s]["taps_lo"][:, 0 : 2 * freq]
        taps_grad = taps_grad + dot(taps_hi, high) + dot(taps_lo, high) + dot(taps_hi, rest)
    small[...] = taps_grad

    def total8(at):
        return jnp.sum(sums8[at : at + 8, :], axis=0, keepdims=True)

    small[49:50, :] = total8(0)
    small[50:51, :] = total8(8) * 0.5
    small[51:52, :] = total8(16) * 0.5
    small[52:53, :] = total8(24) * (scale * drop)
    small[53:54, :] = total8(32) * (0.5 * drop)
    hid = 0.5 * up_grad[width : width + 1, :]
    for k in range(hidden // width):
        small[54 + k : 55 + k, :] = hid[:, k * width : (k + 1) * width]
    for d in range(small_out.shape[0]):
        row = d * count // width
        for k in range(span):
            small_out[d, :, k * width : (k + 1) * width] = small[row + k : row + k + 1, :]
    for copy in grad_copies:
        copy.wait()
    for b in range(max(images - 2, 0), images):
        for copy in out_copies(b, b % 2):
            copy.wait()


def small_bias(rows, start, count, width):
    parts = []
    while count > 0:
        row, col = divmod(start, width)
        size = min(count, width - col)
        parts.append(rows[54 + row : 55 + row, col : col + size])
        start, count = start + size, count - size
    return parts[0] if len(parts) == 1 else jnp.concatenate(parts, axis=1)


def run_block(images, cotangent, group_ids, keep_mask, first, up_t, down, devices, small_count):
    act, normed, inv, spectra, taps, rows = first
    count, extent, _, width = images.shape
    pixels = extent * extent
    hidden = up_t.shape[0]
    span = small_span(small_count, width)
    rows_f = spectrum_rows(extent)
    groups = [make_tables(side, extent, rows_f) for side in SIDES]
    shapes = [(side, g["compact"], g["freq"], g["wide"]) for side, g in zip(SIDES, groups)]
    names, flat = [], []
    for group in groups:
        tables = {"into": low_table(group["into"]), "back": low_table(group["back"])}
        tables["taps_hi"], tables["taps_lo"] = split_table(group["taps"])
        if group["wide"] < pixels:
            tables["pick"] = low_table(group["pick"])
            tables["spread"] = low_table(group["spread"])
        names.append(tuple(tables))
        flat += [jnp.asarray(table) for table in tables.values()]
    capacity = count * pixels + BLOCK
    vmem = pl.BlockSpec(memory_space=pltpu.VMEM)
    smem = pl.BlockSpec(memory_space=pltpu.SMEM)
    hbm = pl.BlockSpec(memory_space=pltpu.HBM)
    scratch = [
        pltpu.VMEM((count, pixels, width), BF),
        pltpu.VMEM((count, pixels, width), BF),
        pltpu.VMEM((capacity, width), BF),
        pltpu.VMEM((capacity, width), BF),
        pltpu.VMEM((capacity, 128), F32),
        pltpu.VMEM((capacity, width), BF),
        pltpu.VMEM(spectra.shape, BF),
        pltpu.VMEM(taps.shape, F32),
        pltpu.VMEM((hidden, width), BF),
        pltpu.VMEM((hidden, width), BF),
        pltpu.VMEM((width + 16, hidden), F32),
        pltpu.VMEM((width, hidden), F32),
        pltpu.VMEM((hidden, width), BF),
        pltpu.VMEM((hidden, width), BF),
        pltpu.VMEM((2, pixels, width), BF),
        pltpu.VMEM((2, pixels, width), F32),
        pltpu.VMEM((2 * rows_f, width), F32),
        pltpu.VMEM((pixels, width), F32),
        pltpu.VMEM((2 * rows_f, width), BF),
        pltpu.VMEM((BLOCK, hidden), BF),
        pltpu.VMEM((BLOCK, hidden), BF),
        pltpu.VMEM((width + 16, BLOCK), BF),
        pltpu.VMEM((BLOCK, width), BF),
        pltpu.VMEM((width, BLOCK), BF),
        pltpu.VMEM((CHUNK, CHUNK), BF),
        pltpu.VMEM((40, width), F32),
        pltpu.VMEM((64, width), F32),
    ]
    scratch += [pltpu.VMEM(table.shape, table.dtype) for table in flat]
    scratch += [pltpu.VMEM((2 * shape[2], width), F32) for shape in shapes]
    scratch += [
        pltpu.SemaphoreType.DMA((count,)),
        pltpu.SemaphoreType.DMA((count,)),
        pltpu.SemaphoreType.DMA((3, count)),
        pltpu.SemaphoreType.DMA((count,)),
        pltpu.SemaphoreType.DMA((5,)),
        pltpu.SemaphoreType.DMA((2, 2)),
        pltpu.SemaphoreType.DMA((len(flat),)),
    ]
    work = 6 * 2 * count * pixels * width * hidden
    return pl.pallas_call(
        partial(block_kernel, shapes, names, rows_f, extent, small_count, span),
        out_shape=(
            jax.ShapeDtypeStruct((count, pixels, width), BF),
            jax.ShapeDtypeStruct((count, pixels, width), F32),
            jax.ShapeDtypeStruct((hidden, width), BF),
            jax.ShapeDtypeStruct((hidden, width), BF),
            jax.ShapeDtypeStruct((devices, 1, span * width), F32),
        ),
        in_specs=[smem, smem] + [hbm] * 9 + [vmem] + [hbm] * len(flat),
        out_specs=(hbm, hbm, hbm, hbm, vmem),
        scratch_shapes=scratch,
        compiler_params=pltpu.CompilerParams(vmem_limit_bytes=VMEM_LIMIT),
        cost_estimate=pl.CostEstimate(flops=work, bytes_accessed=30000000, transcendentals=0),
        name="block",
    )(
        group_ids,
        keep_mask,
        images.reshape(count, pixels, width),
        cotangent.reshape(count, pixels, width),
        act,
        normed,
        inv,
        spectra,
        taps,
        up_t,
        down,
        rows,
        *flat,
    )


def adam_update(weight, moment, second, grad, rate, decay):
    first = beta_one * moment + (1.0 - beta_one) * grad
    second_new = beta_two * second + (1.0 - beta_two) * grad * grad
    step_dir = (
        first / (1.0 - beta_one**STEP) / (jnp.sqrt(second_new / (1.0 - beta_two**STEP)) + adam_eps)
    )
    return (weight - rate * (step_dir + decay * weight), first, second_new)


def wide_split(wide):
    chips = wide // 2
    high = 1
    while high * high < chips:
        high *= 2
    return high, chips // high


AXES = "hlcn"
GATHER_ROUTES = ("nhl", "lnh", "hln")
SCATTER_ROUTES = ("lhn", "hnl", "nlh")


class Place:
    def __init__(self, wide, narrow):
        high, low = wide_split(wide)
        self.sizes = dict(h=high, l=low, c=2, n=narrow)
        spot = lax.axis_index("wide")
        self.at = dict(
            h=spot // (2 * low),
            l=lax.rem(spot // 2, low),
            c=lax.rem(spot, 2),
            n=lax.axis_index("narrow"),
        )

    def shifted(self, axis, step):
        return lax.rem(self.at[axis] + step, self.sizes[axis])

    def device(self, axis, step):
        at = dict(self.at)
        at[axis] = self.shifted(axis, step)
        wide = (at["h"] * self.sizes["l"] + at["l"]) * 2 + at["c"]
        return {"wide": wide, "narrow": at["n"]}

    def peers(self):
        return [(axis, k) for axis in AXES for k in range(1, self.sizes[axis])]

    def greet(self):
        for axis, k in self.peers():
            pl.semaphore_signal(
                pltpu.get_barrier_semaphore(),
                inc=1,
                device_id=self.device(axis, k),
                device_id_type=pl.DeviceIdType.MESH,
            )

    def met(self):
        pl.semaphore_wait(pltpu.get_barrier_semaphore(), len(self.peers()))


def send(src, dst, sems, number, device):
    copy = pltpu.make_async_remote_copy(
        src_ref=src,
        dst_ref=dst,
        send_sem=sems[0].at[number],
        recv_sem=sems[1].at[number],
        device_id=device,
        device_id_type=pl.DeviceIdType.MESH,
    )
    copy.start()
    return copy


def make_parts(spaced, routes):
    tiles = spaced // 16
    cut = 16 * ((2 * tiles + 2) // 3)
    parts = [(2, (0, 1), routes[1]), (0, (0, spaced), routes[0]), (1, (0, cut), routes[1])]
    if cut < spaced:
        parts.append((1, (cut, spaced), routes[2]))
    return parts


def in_order(count, phases):
    return [(p, phase) for phase in range(phases) for p in range(count)]


def gather_copies(sizes):
    count = 1
    for axis in "hln":
        count += 2 * (sizes[axis] - 1)
    return count


def small_span(count, width):
    return (width + count - 2) // width + 1


def small_shift(wide, narrow, count, width):
    device = lax.axis_index("wide") * narrow + lax.axis_index("narrow")
    return lax.rem(device * count, width)


def gather_kernel(wide, narrow, parts, rows_f, *refs):
    refs = list(refs)

    def take(number):
        got = refs[:number]
        del refs[:number]
        return got

    gid = take(1)[0]
    far, img_hbm, far_tables = take(3), take(1)[0], take(3)
    up_hbm, down_hbm, rows, far_first = take(2) + [take(1)[0], take(5)]
    near, tables, bufs = take(3), take(3), take(3)
    img, xhat, act, normed, inv, spectra, taps_f = take(7)
    work, prod, rows_low, small_row = take(4)
    sem_in, sem_img, sem_tables, sem_first, sem_mats, send_sem, recv_sem = take(7)
    into, back, taps_in = tables
    place = Place(wide, narrow)
    here = tuple(place.at[axis] for axis in AXES)
    images, pixels, width = img.shape
    place.greet()
    fetch = [pltpu.make_async_copy(far[w], near[w], sem_in.at[w]) for w in range(3)]
    for copy in fetch:
        copy.start()
    fetch_tables = [
        pltpu.make_async_copy(far_tables[k], tables[k], sem_tables.at[k]) for k in range(3)
    ]

    def img_copy(b):
        return pltpu.make_async_copy(img_hbm.at[b], img.at[b], sem_img.at[b])

    for copy in fetch:
        copy.wait()
    fetch_tables[0].start()
    for b in range(images):
        img_copy(b).start()
    for copy in fetch_tables[1:]:
        copy.start()
    own, count = near[0].shape[0], near[2].shape[0]
    spaced = bufs[0].shape[4]
    for w in range(2):
        if own < spaced:
            bufs[w][here] = jnp.zeros(bufs[w].shape[4:], BF)
        bufs[w][here + (slice(0, own),)] = near[w][...].astype(BF)
    small_row[...] = jnp.zeros_like(small_row)
    small_row[:, 0:count] = near[2][...].reshape(1, count).astype(BF).astype(F32)
    bufs[2][here] = pltpu.roll(small_row[...], small_shift(wide, narrow, count, width), 1)
    place.met()
    sems = (send_sem, recv_sem)
    have = [dict(place.at) for _ in parts]
    started, sibling = [], []
    waiting = [None] * len(parts)
    passed = [[] for _ in parts]

    def region(p):
        which, bounds, _ = parts[p]
        return bufs[which].at[tuple(have[p][axis] for axis in AXES) + (slice(*bounds),)]

    def send_phase(p, phase):
        which, bounds, route = parts[p]
        axis = route[phase]
        waiting[p] = []
        for k in range(1, place.sizes[axis]):
            part = region(p)
            number = len(started) + len(sibling)
            waiting[p].append(send(part, part, sems, number, place.device(axis, k)))
            started.append(waiting[p][-1])

    def pass_over(p):
        number = len(started) + len(sibling)
        part = region(p)
        copy = send(part, part, sems, number, place.device("c", 1))
        sibling.append(copy)
        passed[p].append(copy)

    def finish_phase(p, phase):
        axis = parts[p][2][phase]
        for copy in waiting[p]:
            copy.wait_recv()
        before = have[p]
        have[p] = dict(before)
        have[p][axis] = slice(None)
        after = have[p]
        if phase < 2:
            send_phase(p, phase + 1)
        if phase == 0:
            pass_over(p)
        else:
            for k in range(1, place.sizes[axis]):
                have[p] = dict(before)
                have[p][axis] = place.shifted(axis, k)
                pass_over(p)
            have[p] = after

    def spectrum(b, carry):
        img_copy(b).wait()
        value = dot(into[gid[b], :, 0:pixels], img[b])
        xhat[b] = value
        spectra[b] = value.astype(BF)
        return carry

    def first_copies(b):
        pairs = zip((act, normed, inv, spectra), far_first)
        return [
            pltpu.make_async_copy(close.at[b], away.at[b], sem_first.at[k, b])
            for k, (close, away) in enumerate(pairs)
        ]

    def convolve(b, carry):
        g = gid[b]
        for r, size in strips(rows_f, 48):
            lo, hi = slice(r, r + size), slice(rows_f + r, rows_f + r + size)
            re, im = xhat[b, lo, :], xhat[b, hi, :]
            t_re, t_im = taps_f[g, lo, :], taps_f[g, hi, :]
            prod[lo, :] = (re * t_re - im * t_im).astype(BF)
            prod[hi, :] = (re * t_im + im * t_re).astype(BF)
        work[...] = dot(back[g, :, 0 : 2 * rows_f], prod[...])
        conv_bias, gain, norm_bias = rows[49:50, :], rows[50:51, :], rows[51:52, :]
        for r, size in strips(pixels, 64):
            span = slice(r, r + size)
            conv = work[span, :] + conv_bias
            center = conv - jnp.mean(conv, axis=1, keepdims=True)
            scale = lax.rsqrt(jnp.mean(center * center, axis=1, keepdims=True) + 1e-06)
            value = center * scale
            normed[b, span, :] = value.astype(BF)
            inv[b, span, :] = jnp.broadcast_to(scale, (size, 128))
            act[b, span, :] = (value * gain + norm_bias).astype(BF)
        for copy in first_copies(b):
            copy.start()
        return carry

    big = range(1, len(parts))
    ahead = max(images - 3, 0)
    for p in range(len(parts)):
        send_phase(p, 0)
    fetch_tables[0].wait()
    lax.fori_loop(0, images // 4, spectrum, 0)
    for p in range(len(parts)):
        finish_phase(p, 0)
    lax.fori_loop(images // 4, images // 2, spectrum, 0)
    finish_phase(0, 1)
    lax.fori_loop(images // 2, 3 * images // 4, spectrum, 0)
    finish_phase(0, 2)
    for p in big:
        finish_phase(p, 1)
    lax.fori_loop(3 * images // 4, images, spectrum, 0)
    for copy in fetch_tables[1:]:
        copy.wait()
    for copy in passed[0]:
        copy.wait_recv()
    collect_rows(bufs[2], count, rows)
    rows_low[0:64, :] = rows[...].astype(BF)
    rows_low[64:128, :] = rows[...].astype(BF)
    for s in range(3):
        taps_f[s] = dot(taps_in[s], rows_low[...])
    taps_copy = pltpu.make_async_copy(taps_f, far_first[4], sem_mats.at[2])
    taps_copy.start()
    lax.fori_loop(0, ahead, convolve, 0)
    for p in big:
        finish_phase(p, 2)
    lax.fori_loop(ahead, images - 1, convolve, 0)
    for p in big:
        for copy in passed[p]:
            copy.wait_recv()
    mats = [
        pltpu.make_async_copy(bufs[0], up_hbm, sem_mats.at[0]),
        pltpu.make_async_copy(bufs[1], down_hbm, sem_mats.at[1]),
    ]
    for copy in mats:
        copy.start()
    lax.fori_loop(images - 1, images, convolve, 0)

    def settle(b, carry):
        for copy in first_copies(b):
            copy.wait()
        return carry

    lax.fori_loop(0, images, settle, 0)
    for copy in mats:
        copy.wait()
    taps_copy.wait()
    for copy in started + sibling:
        copy.wait_send()


def collect_rows(pieces, count, rows):
    high, low, cores, narrow = pieces.shape[:4]
    width = rows.shape[1]
    terms = [[] for _ in range(rows.shape[0])]
    for d in range(high * low * cores * narrow):
        spot = (d // (low * cores * narrow), d // (cores * narrow) % low, d // narrow % cores, d % narrow)
        first, final = d * count // width, (d * count + count - 1) // width
        for r in range(first, final + 1):
            terms[r].append(pieces[spot][:, (r - first) * width : (r - first + 1) * width])
    for r, parts in enumerate(terms):
        value = jnp.zeros((1, width), F32)
        for part in parts:
            value = value + part
        rows[r : r + 1, :] = value


def gather_weights(wide, narrow, weights, images, group_ids):
    up, down, small = weights
    high, low = wide_split(wide)
    sizes = dict(h=high, l=low, n=narrow)
    own, width = up.shape
    images_n, extent = images.shape[:2]
    pixels = extent * extent
    count = small.shape[0]
    spaced = round_up(own, 16)
    lanes = small_span(count, width) * width
    grid = (high, low, 2, narrow)
    rows_f = spectrum_rows(extent)
    hbm = pl.BlockSpec(memory_space=pltpu.HBM)
    smem = pl.BlockSpec(memory_space=pltpu.SMEM)
    parts = make_parts(spaced, GATHER_ROUTES)
    copies = len(parts) * gather_copies(sizes)
    groups = [make_tables(side, extent, rows_f) for side in SIDES]
    tables = [
        low_table(np.stack([g["first_into"] for g in groups])),
        low_table(np.stack([g["first_back"] for g in groups])),
        stacked_split(np.stack([g["first_taps"] for g in groups])),
    ]
    first = [
        jax.ShapeDtypeStruct((images_n, pixels, width), BF),
        jax.ShapeDtypeStruct((images_n, pixels, width), BF),
        jax.ShapeDtypeStruct((images_n, pixels, 128), F32),
        jax.ShapeDtypeStruct((images_n, 2 * rows_f, width), BF),
        jax.ShapeDtypeStruct((3, 2 * rows_f, width), F32),
    ]
    bufs = [
        jax.ShapeDtypeStruct(grid + (spaced, width), BF),
        jax.ShapeDtypeStruct(grid + (spaced, width), BF),
        jax.ShapeDtypeStruct(grid + (1, lanes), F32),
    ]
    near = [
        pltpu.VMEM((own, width), F32),
        pltpu.VMEM((own, width), F32),
        pltpu.VMEM((count,), F32),
    ]
    scratch = near + [pltpu.VMEM(table.shape, BF) for table in tables]
    scratch += [pltpu.VMEM(buf.shape, buf.dtype) for buf in bufs]
    scratch += [
        pltpu.VMEM((images_n, pixels, width), BF),
        pltpu.VMEM((images_n, 2 * rows_f, width), F32),
    ]
    scratch += [pltpu.VMEM(part.shape, part.dtype) for part in first]
    scratch += [
        pltpu.VMEM((pixels, width), F32),
        pltpu.VMEM((2 * rows_f, width), BF),
        pltpu.VMEM((128, width), BF),
        pltpu.VMEM((1, lanes), F32),
        pltpu.SemaphoreType.DMA((3,)),
        pltpu.SemaphoreType.DMA((images_n,)),
        pltpu.SemaphoreType.DMA((4,)),
        pltpu.SemaphoreType.DMA((4, images_n)),
        pltpu.SemaphoreType.DMA((3,)),
        pltpu.SemaphoreType.DMA((copies,)),
        pltpu.SemaphoreType.DMA((copies,)),
    ]
    out = pl.pallas_call(
        partial(gather_kernel, wide, narrow, parts, rows_f),
        out_shape=tuple(bufs[:2] + [jax.ShapeDtypeStruct((64, width), F32)] + first),
        in_specs=[smem] + [hbm] * 7,
        out_specs=(hbm, hbm, pl.BlockSpec(memory_space=pltpu.VMEM)) + (hbm,) * 5,
        scratch_shapes=scratch,
        compiler_params=pltpu.CompilerParams(
            collective_id=0, has_side_effects=True, vmem_limit_bytes=VMEM_LIMIT
        ),
        name="gather",
    )(
        group_ids,
        up,
        down,
        small,
        images.reshape(images_n, pixels, width),
        *[jnp.asarray(table) for table in tables],
    )
    return out[0], out[1], out[3:] + (out[2],)


def scatter_shapes(sizes, parts, spaced, width, lanes):
    shapes = []
    for which, bounds, route in parts:
        tail, dtype = ((bounds[1] - bounds[0], width), BF) if which < 2 else ((1, lanes), F32)
        left = dict(h=sizes["h"], l=sizes["l"], n=sizes["n"])
        shapes.append(pltpu.VMEM(tuple(left.values()) + tail, dtype))
        for axis in route:
            del left[axis]
            shapes.append(
                pltpu.VMEM((max(sizes[axis] - 1, 1),) + tuple(left.values()) + tail, dtype)
            )
    return shapes


def scatter_kernel(wide, narrow, parts, *refs):
    refs = list(refs)

    def take(count):
        got = refs[:count]
        del refs[:count]
        return got

    far = take(3)
    sums_out = take(3)
    own, sums = take(3), take(3)
    landing = [take(4) for _ in parts]
    sem_own, send_sem, recv_sem = take(3)
    sems = (send_sem, recv_sem)
    place = Place(wide, narrow)
    place.greet()
    at, sizes = place.at, place.sizes
    full = slice(None)
    fetch = [
        pltpu.make_async_copy(far[w].at[full, full, at["c"]], own[w], sem_own.at[w])
        for w in range(3)
    ]
    for copy in fetch:
        copy.start()
    place.met()
    started = []
    for p, (which, bounds, route) in enumerate(parts):
        src = far[which].at[full, full, 1 - at["c"], full, slice(*bounds)]
        started.append(send(src, landing[p][0], sems, len(started), place.device("c", 1)))
    waiting = [[copy] for copy in started]
    left = [dict(h=full, l=full, n=full) for _ in parts]

    def spot(fixed):
        return tuple(fixed[axis] for axis in "hln")

    def send_phase(p, phase):
        which, bounds, route = parts[p]
        axis = route[phase]
        waiting[p] = []
        for k in range(1, sizes[axis]):
            there = dict(left[p])
            there[axis] = place.shifted(axis, k)
            src = sums[which].at[spot(there) + (slice(*bounds),)]
            dst = landing[p][1 + phase].at[k - 1]
            copy = send(src, dst, sems, len(started), place.device(axis, k))
            waiting[p].append(copy)
            started.append(copy)

    for copy in fetch:
        copy.wait()
    for p, phase in in_order(len(parts), 4):
        which, bounds, route = parts[p]
        rows = slice(*bounds)
        for copy in waiting[p]:
            copy.wait_recv()
        if phase == 0:
            for h in range(sizes["h"]):
                for l in range(sizes["l"]):
                    both = own[which][h, l, :, rows].astype(F32) + landing[p][0][h, l].astype(F32)
                    sums[which][h, l, :, rows] = both.astype(sums[which].dtype)
            send_phase(p, 0)
            continue
        axis = route[phase - 1]
        left[p][axis] = at[axis]
        target = spot(left[p]) + (rows,)
        total = sums[which][target].astype(F32)
        for k in range(1, sizes[axis]):
            total = total + landing[p][phase][k - 1].astype(F32)
        if phase < 3:
            sums[which][target] = total.astype(sums[which].dtype)
            send_phase(p, phase)
        else:
            sums_out[which][rows] = total
    for copy in started:
        copy.wait_send()


def scatter_sums(wide, narrow, partials):
    high, low = wide_split(wide)
    sizes = dict(h=high, l=low, n=narrow)
    spaced, width = partials[0].shape[4:]
    lanes = partials[2].shape[5]
    parts = make_parts(spaced, SCATTER_ROUTES)
    copies = len(parts) * (1 + sum(sizes[axis] - 1 for axis in "hln"))
    hbm = pl.BlockSpec(memory_space=pltpu.HBM)
    vmem = pl.BlockSpec(memory_space=pltpu.VMEM)
    grid = (high, low, narrow)
    halves = [
        pltpu.VMEM(grid + (spaced, width), BF),
        pltpu.VMEM(grid + (spaced, width), BF),
        pltpu.VMEM(grid + (1, lanes), F32),
    ]
    scratch = halves + halves + scatter_shapes(sizes, parts, spaced, width, lanes)
    scratch += [
        pltpu.SemaphoreType.DMA((3,)),
        pltpu.SemaphoreType.DMA((copies,)),
        pltpu.SemaphoreType.DMA((copies,)),
    ]
    return pl.pallas_call(
        partial(scatter_kernel, wide, narrow, parts),
        out_shape=(
            jax.ShapeDtypeStruct((spaced, width), F32),
            jax.ShapeDtypeStruct((spaced, width), F32),
            jax.ShapeDtypeStruct((1, lanes), F32),
        ),
        in_specs=[hbm] * 3,
        out_specs=(vmem,) * 3,
        scratch_shapes=scratch,
        compiler_params=pltpu.CompilerParams(
            collective_id=1, has_side_effects=True, vmem_limit_bytes=VMEM_LIMIT
        ),
        name="scatter",
    )(*partials)


def update_kernel(wide, narrow, width, *refs):
    grads, weights, moments, seconds = refs[0:3], refs[3:6], refs[6:9], refs[9:12]
    news, firsts, nexts, lows = refs[12:15], refs[15:18], refs[18:21], refs[21:24]
    for which in range(3):
        shape = weights[which].shape
        if which < 2:
            grad = grads[which][0 : shape[0], :]
        else:
            lanes = grads[which].shape[1]
            shift = lanes - small_shift(wide, narrow, shape[0], width)
            grad = pltpu.roll(grads[which][...], shift, 1)[:, 0 : shape[0]]

        def flat(value):
            return value if which < 2 else value.reshape(1, shape[0])

        rate, decay = (rate_mats, decay_mats) if which < 2 else (rate_small, 0.0)
        new, first, second = adam_update(
            flat(weights[which][...]),
            flat(moments[which][...]),
            flat(seconds[which][...]),
            grad,
            rate,
            decay,
        )
        news[which][...] = new.reshape(shape)
        firsts[which][...] = first.reshape(shape)
        nexts[which][...] = second.reshape(shape)
        lows[which][...] = new.reshape(shape).astype(BF)


def update(wide, narrow, grads, weights, moments, seconds):
    like = [jax.ShapeDtypeStruct(weight.shape, F32) for weight in weights]
    low = [jax.ShapeDtypeStruct(weight.shape, BF) for weight in weights]
    vmem = pl.BlockSpec(memory_space=pltpu.VMEM)
    return pl.pallas_call(
        partial(update_kernel, wide, narrow, weights[0].shape[1]),
        out_shape=tuple(like * 3 + low),
        in_specs=[vmem] * 12,
        out_specs=(vmem,) * 12,
        compiler_params=pltpu.CompilerParams(vmem_limit_bytes=VMEM_LIMIT),
        name="update",
    )(*grads, *weights, *moments, *seconds)


def per_device(
    wide,
    narrow,
    images,
    cotangent,
    group_ids,
    keep_mask,
    up_weight,
    down_weight,
    small_params,
    up_moment,
    down_moment,
    small_moment,
    up_second,
    down_second,
    small_second,
):
    width = images.shape[3]
    own, count = down_weight.shape[0], small_params.shape[0]
    devices = wide * narrow

    def laid(three):
        return three[0].T, three[1], three[2]

    weights = laid((up_weight, down_weight, small_params))
    moments = laid((up_moment, down_moment, small_moment))
    seconds = laid((up_second, down_second, small_second))
    gu, gd, first = gather_weights(wide, narrow, weights, images, group_ids)
    grid, spaced = gu.shape[:4], gu.shape[4]

    def dense(blocks):
        return blocks.reshape(devices, spaced, width)[:, :own].reshape(devices * own, width)

    def spread(rows):
        rows = rows.reshape(devices, own, width)
        return jnp.pad(rows, ((0, 0), (0, spaced - own), (0, 0))).reshape(
            grid + (spaced, width)
        )

    activations, input_grad, up_part, down_part, small_part = run_block(
        images, cotangent, group_ids, keep_mask, first, dense(gu), dense(gd), devices, count
    )
    small_part = small_part.reshape(grid + small_part.shape[1:])
    grads = scatter_sums(wide, narrow, (spread(up_part), spread(down_part), small_part))
    out = update(wide, narrow, grads, weights, moments, seconds)
    groups = [(out[k].T, out[k + 1], out[k + 2]) for k in range(0, 12, 3)]
    maps = (activations.reshape(images.shape), input_grad.reshape(images.shape))
    return maps + groups[0] + groups[1] + groups[2] + groups[3]


def solution(mesh):
    both = ("wide", "narrow")
    maps = P(both, None, None, None)
    cols, rows, flat = P(None, both), P(both, None), P(both)
    three = (cols, rows, flat)
    return jax.shard_map(
        partial(per_device, mesh.shape["wide"], mesh.shape["narrow"]),
        mesh=mesh,
        in_specs=(maps, maps, flat, flat) + three * 3,
        out_specs=(maps, maps) + three * 4,
        check_vma=False,
    )
```

time: 973 us -> 113 us (0.12); the launches traced: 962 us -> 114 us
  other arithmetic: 560 us -> 0 us
  matrix products: 146 us -> 0 us
  waiting for transfers between devices: 121 us -> 0 us
  Pallas kernels: 0 us -> 113 us
  local copies, waits for them, and re-layouts: 78.1 us -> 0 us
  blocking collectives: 42.5 us -> 0 us
  between operations: 15.3 us -> 0.82 us
    reduce_sum x7 -> x0, other arithmetic: 363 us -> none  [the longest x1 202 us: per_device(): center = conv - jnp.mean(conv, axis=-1, keepdims=True)]
    add x1 -> x0, other arithmetic: 181 us -> none  [per_device(): input_grad = upstream + valid * back_total]
    dot_general x6 -> x0, matrix products: 146 us -> none  [the longest x1 69.4 us: per_device(): jnp.dot(act, full_up, preferred_element_type=jnp.float32)]
    reduce_scatter x2 -> x0, waiting for transfers between devices: 121 us -> none  [the longest x1 102 us: per_device(): lax.psum_scatter(up_grad, ('wide', 'narrow'), scatter_dimension=1, tiled=...]
    pallas_call x0 -> x4, Pallas kernels: none -> 113 us  [the longest x1 56.7 us: run_block(): pl.pallas_call(partial(block_kernel, shapes, names, rows_f, extent, small...]
    another operation x54 -> x0, local copies, waits for them, and re-layouts: 61.9 us -> none  [the longest x49 58.4 us: per_device(): jnp.stack(tap_grads)]
    unnamed x1 -> x0, blocking collectives: 42.5 us -> none
    concatenate x1 -> x0, local copies, waits for them, and re-layouts: 10.6 us -> none  [per_device(): jnp.concatenate([jnp.stack(tap_grads), jnp.stack([convb_grad, gain_grad,...]
  transfers between devices with their start and end apart: 5 -> 0, of which waited for: 2 -> 0; matrix products, arithmetic and copies ran while one was open for 52% -> 0% of each run, Pallas kernels for 0% -> 0%
where the time goes in v1:
time: 113 us; the launch traced here: 114 us
  Pallas kernels  113 us (100%)
    pallas_call x1, Pallas kernels, run_block(): pl.pallas_call(partial(block_kernel, shapes, names, rows_f, extent, small...  56.7 us
    pallas_call x1, Pallas kernels, gather_weights(): pl.pallas_call(partial(gather_kernel, wide, narrow, parts, rows_f), out_s...  29.2 us
    pallas_call x1, Pallas kernels, scatter_sums(): pl.pallas_call(partial(scatter_kernel, wide, narrow, parts), out_shape=(j...  24.8 us

profile of v1, /device:TPU:0, one launch (start us, length us, event | category | flops | bytes accessed | tf_op | source)
XLA Modules:
  0.0 113.6 jit_solution(13370340758367310648)
XLA Ops:
  0.6 29.2 %gather.1 = (bf16[2,2,2,4,48,384]{5,4,3,2,1,0:T(8,128)(2,1)}, bf16[2,2,2,4,48,384]{5,4,3,2,1,0:T(8,128)(2,1)}, f32[64,384]{1,0:T(8,128)}, bf16[8,576,384]{2,1,0:...) custom-call(s32[8]{0:T(128)} %refs_0_.3, ...), custom_call_target="tpu_custom_call" | custom-call | tf_op jit(solution)/shard_map/gather/pallas_call | solution.py:911
  29.9 56.7 %block.1 = (bf16[8,576,384]{2,1,0:T(8,128)(2,1)}, f32[8,576,384]{2,1,0:T(8,128)}, bf16[1536,384]{1,0:T(8,128)(2,1)}, bf16[1536,384]{1,0:T(8,128)(2,1)}, f32[32,1,1152]{2,1,0:T(1,128)}) custom-call(s32[8]{0:T(128)} %refs_0_.3, s32[8]{0:T(128)} %refs_1_.1, bf16[8,576,384]{2,1,0:T(8,128)(2,1)} %bitcast.17, bf16[8,576,384]{2,1,0:T(8,128)(2,1)} %bitcast.25, ...), custom_call_target="tpu_custom_call" | custom-call | flops 32614907904 | bytes 30000000 | tf_op jit(solution)/shard_map/block/pallas_call | solution.py:519
  86.6 24.8 %scatter.1 = (f32[48,384]{1,0:T(8,128)}, f32[48,384]{1,0:T(8,128)}, f32[1,1152]{1,0:T(1,128)}) custom-call(bf16[2,2,2,4,48,384]{5,4,3,2,1,0:T(8,128)(2,1)} %bitcast.18, bf16[2,2,2,4,48,384]{5,4,3,2,1,0:T(8,128)(2,1)} %bitcast.19, f32[2,2,2,4,1,1152]{5,4,3,2,1,0:T(1,128)} %bitcast.22), custom_call_target="tpu_custom_call" | custom-call | tf_op jit(solution)/shard_map/scatter/pallas_call | solution.py:1044
  111.4 2.1 %update.1 = (f32[48,384]{1,0:T(8,128)}, f32[48,384]{1,0:T(8,128)}, f32[696]{0:T(1024)}, f32[48,384]{1,0:T(8,128)}, f32[48,384]{1,0:T(8,128)}, /*index=5*/f32[696...) custom-call(f32[48,384]{1,0:T(8,128)} %get-tuple-element.55.refs_0_,, ...), custom_call_target="tpu_custom_call" | custom-call | tf_op jit(solution)/shard_map/update/pallas_call | solution.py:1095

commit v2 on v1

--- a/solution.py
+++ b/solution.py
@@ -114,7 +114,7 @@
 def twice_gelu(pre):
     part = pre * 0.7071067811865476
     level = 1.0 + lax.erf(part)
-    bell = (pre * 0.7978845608028654) * jnp.exp2(part * part * -1.4426950408889634)
+    bell = (pre * 0.7978845608028654) * jnp.exp(-(part * part))
     return pre * level, level + bell
 
 
@@ -135,7 +135,7 @@
     far_tables = [take(len(group)) for group in names]
     act_hbm, ig_hbm, up_out, down_out, small_out = take(5)
     img, cot, act_rows, normed_rows, inv_rows, cot_rows, spectra, taps_f = take(8)
-    up_t, down, up_grad, down_grad, up_low, down_low = take(6)
+    up_t, down, up_c, down_c, up_grad, down_grad, up_low, down_low = take(8)
     act_out, ig_out, work_a, work_b, prod = take(5)
     post_s, prg_s, act_t, pg_s, pg_t, eye, sums8, small = take(8)
     near_tables = [take(len(group)) for group in names]
@@ -232,6 +232,10 @@
     inv_rows[pl.ds(end, BLOCK), :] = jnp.zeros((BLOCK, 128), F32)
     for copy in mat_copies:
         copy.wait()
+    for h in range(0, hidden, CHUNK):
+        cols = slice(h, h + CHUNK)
+        up_c[:, cols] = up_t[cols, :].T
+        down_c[:, cols] = down[cols, :].T
     for k in early:
         table_copies[k].wait()
 
@@ -253,8 +257,8 @@
                 post_s[span, cols] = post.astype(BF)
                 pull = back_all[span] * slope
                 prg_s[span, cols] = pull.astype(BF)
-        proj = dot(post_s[...], down[...])
-        act_grad = dot(prg_s[...], up_t[...])
+        proj = dot_t(down_c[...], post_s[...]).T
+        act_grad = dot_t(up_c[...], prg_s[...]).T
         for h in range(0, hidden, CHUNK):
             cols = slice(h, h + CHUNK)
             down_grad[:, cols] += dot(pg_t[...], post_s[:, cols])
@@ -486,6 +490,8 @@
         pltpu.VMEM(taps.shape, F32),
         pltpu.VMEM((hidden, width), BF),
         pltpu.VMEM((hidden, width), BF),
+        pltpu.VMEM((width, hidden), BF),
+        pltpu.VMEM((width, hidden), BF),
         pltpu.VMEM((width + 16, hidden), F32),
         pltpu.VMEM((width, hidden), F32),
         pltpu.VMEM((hidden, width), BF),
@@ -791,9 +797,9 @@
     finish_phase(0, 1)
     lax.fori_loop(images // 2, 3 * images // 4, spectrum, 0)
     finish_phase(0, 2)
+    lax.fori_loop(3 * images // 4, images, spectrum, 0)
     for p in big:
         finish_phase(p, 1)
-    lax.fori_loop(3 * images // 4, images, spectrum, 0)
     for copy in fetch_tables[1:]:
         copy.wait()
     for copy in passed[0]:

time: 113 us -> 110 us (0.973); the launches traced: 114 us -> 109 us
  Pallas kernels: 113 us -> 109 us
    pallas_call x1, Pallas kernels: 56.7 us -> 50.1 us  [run_block(): pl.pallas_call(partial(block_kernel, shapes, names, rows_f, extent, small...]
    pallas_call x1, Pallas kernels: 29.2 us -> 30.6 us  [gather_weights(): pl.pallas_call(partial(gather_kernel, wide, narrow, parts, rows_f), out_s...]
where the time goes in v2:
time: 110 us; the launch traced here: 109 us
  Pallas kernels  109 us (99%)
    pallas_call x1, Pallas kernels, run_block(): pl.pallas_call(partial(block_kernel, shapes, names, rows_f, extent, small...  50.1 us
    pallas_call x1, Pallas kernels, gather_weights(): pl.pallas_call(partial(gather_kernel, wide, narrow, parts, rows_f), out_s...  30.6 us
    pallas_call x1, Pallas kernels, scatter_sums(): pl.pallas_call(partial(scatter_kernel, wide, narrow, parts), out_shape=(j...  25.7 us

profile of v2, /device:TPU:0, one launch (start us, length us, event | category | flops | bytes accessed | tf_op | source)
XLA Modules:
  0.0 109.3 jit_solution(1108697744783635998)
XLA Ops:
  0.6 30.6 %gather.1 = (bf16[2,2,2,4,48,384]{5,4,3,2,1,0:T(8,128)(2,1)}, bf16[2,2,2,4,48,384]{5,4,3,2,1,0:T(8,128)(2,1)}, f32[64,384]{1,0:T(8,128)}, bf16[8,576,384]{2,1,0:...) custom-call(s32[8]{0:T(128)} %refs_0_.3, ...), custom_call_target="tpu_custom_call" | custom-call | tf_op jit(solution)/shard_map/gather/pallas_call | solution.py:917
  31.2 50.1 %block.1 = (bf16[8,576,384]{2,1,0:T(8,128)(2,1)}, f32[8,576,384]{2,1,0:T(8,128)}, bf16[1536,384]{1,0:T(8,128)(2,1)}, bf16[1536,384]{1,0:T(8,128)(2,1)}, f32[32,1,1152]{2,1,0:T(1,128)}) custom-call(s32[8]{0:T(128)} %refs_0_.3, s32[8]{0:T(128)} %refs_1_.1, bf16[8,576,384]{2,1,0:T(8,128)(2,1)} %bitcast.17, bf16[8,576,384]{2,1,0:T(8,128)(2,1)} %bitcast.25, ...), custom_call_target="tpu_custom_call" | custom-call | flops 32614907904 | bytes 30000000 | tf_op jit(solution)/shard_map/block/pallas_call | solution.py:525
  81.4 25.7 %scatter.1 = (f32[48,384]{1,0:T(8,128)}, f32[48,384]{1,0:T(8,128)}, f32[1,1152]{1,0:T(1,128)}) custom-call(bf16[2,2,2,4,48,384]{5,4,3,2,1,0:T(8,128)(2,1)} %bitcast.18, bf16[2,2,2,4,48,384]{5,4,3,2,1,0:T(8,128)(2,1)} %bitcast.19, f32[2,2,2,4,1,1152]{5,4,3,2,1,0:T(1,128)} %bitcast.22), custom_call_target="tpu_custom_call" | custom-call | tf_op jit(solution)/shard_map/scatter/pallas_call | solution.py:1050
  107.1 2.1 %update.1 = (f32[48,384]{1,0:T(8,128)}, f32[48,384]{1,0:T(8,128)}, f32[696]{0:T(1024)}, f32[48,384]{1,0:T(8,128)}, f32[48,384]{1,0:T(8,128)}, /*index=5*/f32[696...) custom-call(f32[48,384]{1,0:T(8,128)} %get-tuple-element.55.refs_0_,, ...), custom_call_target="tpu_custom_call" | custom-call | tf_op jit(solution)/shard_map/update/pallas_call | solution.py:1101
